TPU v7x, 128 devices: a whole 4x4x4 slice. The times are simulated.
128 devices in a mesh: ctx: 16 (over y_lo, z, core), tp: 8 (over y_hi, x).
Axes of the slice: x: 4, y: 4 (y_hi: 2, y_lo: 2; y = y_hi * 2 + y_lo), z: 4, core: 2. Of those that a mesh axis runs over, the one named last changes fastest.
Arguments:
- tokens: bfloat16 [4096, 16384], P('tp', 'ctx'), may hold values from -6 to 6
- in_weight: bfloat16 [3, 4096, 4096], P(None, 'ctx', 'tp'), may hold values from -0.09375 to 0.09375
- short_taps: float32 [3, 4096, 3], P(None, 'tp'), may hold values from -3 to 3
- long_filter: float32 [4096, 16384], P('tp', 'ctx'), may hold values from -2 to 2
- skip_gain: float32 [4096], P('tp'), may hold values from -4 to 4
- out_weight: bfloat16 [4096, 4096], P('tp', 'ctx'), may hold values from -0.125 to 0.125
Outputs:
- layer_out: bfloat16 [4096, 16384], P('tp', 'ctx')
All inputs are finite; a program needn't handle non-finite values.
Results may differ from a plain program's by a relative error of at most 0.02.
Values may be sent and summed in bfloat16 or wider, within the bound.
A program may use at most 128 MiB of HBM per device.

v0:
```python
import math

import jax
import jax.numpy as jnp
from jax import lax
from jax.sharding import PartitionSpec as P

HIGHEST = lax.Precision.HIGHEST


def passed_along(shard, axis, by):
    count = lax.axis_size(axis)
    pairs = [(i, i + by) for i in range(count) if 0 <= i + by < count]
    return lax.ppermute(shard, axis, pairs)


def factor_length(full_len):
    inner_len = 1
    while inner_len * inner_len * 4 <= full_len and full_len % (inner_len * 2) == 0:
        inner_len = inner_len * 2
    return (inner_len, full_len // inner_len)


def phase_table(rows_count, cols_count, period):
    row_ids = jnp.arange(rows_count, dtype=jnp.int32)[:, None]
    col_ids = jnp.arange(cols_count, dtype=jnp.int32)[None, :]
    angles = (row_ids * col_ids % period).astype(jnp.float32) * (2.0 * math.pi / period)
    return (jnp.cos(angles), jnp.sin(angles))


def make_tables(full_len):
    inner_len, outer_len = factor_length(full_len)
    cos_inner, sin_inner = phase_table(inner_len, inner_len, inner_len)
    cos_outer, sin_outer = phase_table(outer_len // 2, outer_len, outer_len)
    cos_twist, sin_twist = phase_table(outer_len, inner_len, full_len)
    return (cos_inner, sin_inner, cos_outer, sin_outer, cos_twist, sin_twist)


def spectrum(signal, tables):
    cos_inner, sin_inner, cos_outer, sin_outer, cos_twist, sin_twist = tables
    channels = signal.shape[0]
    grid_view = signal.reshape(channels, cos_outer.shape[0], cos_inner.shape[0])
    part_re = jnp.einsum("cmn,mk->ckn", grid_view, cos_outer, precision=HIGHEST)
    part_im = -jnp.einsum("cmn,mk->ckn", grid_view, sin_outer, precision=HIGHEST)
    twist_re = part_re * cos_twist + part_im * sin_twist
    twist_im = part_im * cos_twist - part_re * sin_twist
    freq_re = jnp.einsum("ckn,nj->ckj", twist_re, cos_inner, precision=HIGHEST) + jnp.einsum(
        "ckn,nj->ckj", twist_im, sin_inner, precision=HIGHEST
    )
    freq_im = jnp.einsum("ckn,nj->ckj", twist_im, cos_inner, precision=HIGHEST) - jnp.einsum(
        "ckn,nj->ckj", twist_re, sin_inner, precision=HIGHEST
    )
    return (freq_re, freq_im)


def spectrum_back(freq_re, freq_im, tables):
    cos_inner, sin_inner, cos_outer, sin_outer, cos_twist, sin_twist = tables
    mix_re = jnp.einsum("ckj,jn->ckn", freq_re, cos_inner, precision=HIGHEST) - jnp.einsum(
        "ckj,jn->ckn", freq_im, sin_inner, precision=HIGHEST
    )
    mix_im = jnp.einsum("ckj,jn->ckn", freq_im, cos_inner, precision=HIGHEST) + jnp.einsum(
        "ckj,jn->ckn", freq_re, sin_inner, precision=HIGHEST
    )
    turn_re = mix_re * cos_twist - mix_im * sin_twist
    turn_im = mix_im * cos_twist + mix_re * sin_twist
    channels = freq_re.shape[0]
    length = cos_outer.shape[0] * cos_inner.shape[0]
    norm_factor = 1.0 / (cos_outer.shape[1] * cos_inner.shape[0])
    real_out = jnp.einsum("ckn,mk->cmn", turn_re, cos_outer, precision=HIGHEST) - jnp.einsum(
        "ckn,mk->cmn", turn_im, sin_outer, precision=HIGHEST
    )
    real_out = real_out.reshape(channels, length) * norm_factor
    return real_out


def per_device(tokens, in_weight, short_taps, long_filter, skip_gain, out_weight):
    steps_dev = tokens.shape[1]
    filter_groups = lax.all_to_all(
        long_filter.astype(jnp.bfloat16), "ctx", split_axis=0, concat_axis=1, tiled=True
    ).astype(long_filter.dtype)
    features_all = lax.all_gather(tokens, "tp", axis=0, tiled=True)
    sources = (features_all,)
    shard_rows = lax.all_gather(in_weight, "ctx", axis=1, tiled=True)
    results = tuple(
        (
            jnp.einsum("sic,it->sct", shard_rows, source, preferred_element_type=jnp.float32)
            for source in sources
        )
    )
    projected = results[0]
    before = passed_along(projected[:, :, steps_dev - 2 :], "ctx", 1)
    prev_one = jnp.concatenate([before[:, :, 1:], projected[:, :, :-1]], axis=2)
    prev_two = jnp.concatenate([before, projected[:, :, :-2]], axis=2)
    mixed_short = (
        short_taps[:, :, 0:1] * projected
        + short_taps[:, :, 1:2] * prev_one
        + short_taps[:, :, 2:3] * prev_two
    )
    gated_rows = (mixed_short[1] * mixed_short[2]).astype(jnp.bfloat16)
    signal = lax.all_to_all(gated_rows, "ctx", split_axis=0, concat_axis=1, tiled=True)
    tables = make_tables(2 * signal.shape[1])
    sig_re, sig_im = spectrum(signal.astype(jnp.float32), tables)
    fil_re, fil_im = spectrum(filter_groups, tables)
    prod_re = sig_re * fil_re - sig_im * fil_im
    prod_im = sig_re * fil_im + sig_im * fil_re
    long_rows = spectrum_back(prod_re, prod_im, tables)
    long_rows = long_rows.astype(jnp.bfloat16)
    returned = lax.all_to_all(long_rows, "ctx", split_axis=1, concat_axis=0, tiled=True)
    hidden = (
        (returned.astype(jnp.float32) + skip_gain[:, None] * gated_rows.astype(jnp.float32))
        * mixed_short[0]
    ).astype(jnp.bfloat16)
    whole_out = lax.all_gather(out_weight, "ctx", axis=1, tiled=True)
    return lax.psum_scatter(
        jnp.einsum("cd,ct->dt", whole_out, hidden, preferred_element_type=jnp.float32).astype(
            jnp.bfloat16
        ),
        "tp",
        scatter_dimension=0,
        tiled=True,
    )


def solution(mesh):
    placed = (
        P("tp", "ctx"),
        P(None, "ctx", "tp"),
        P(None, "tp", None),
        P("tp", "ctx"),
        P("tp"),
        P("tp", "ctx"),
    )
    return jax.shard_map(
        per_device, mesh=mesh, in_specs=placed, out_specs=P("tp", "ctx"), check_vma=False
    )
```

profile of v0, /device:TPU:1, one launch (start us, length us, event | category | flops | bytes accessed | tf_op | source)
XLA Modules:
  0.0 480.2 jit_solution(12676117775673328608)
XLA Ops:
  7.3 2.3 copy.25
  10.8 7.8 %all-to-all-start.1 = ((bf16[16,32,1024]{2,1,0:T(8,128)(2,1)}), bf16[16,32,1024]{2,1,0:T(8,128)(2,1)S(1)}, u32[]{:S(2)}, u32[]{:S(2)}) async-start(bf16[16,32,1024]{2,1,0:T(8,128)(2,1)} %bitcast.11), calls=%async_computation.1 | async-start | bytes 2097152 | tf_op jit(solution)/shard_map/all_to_all | solution.py:78
  20.0 19.7 %all-to-all-done.1 = bf16[16,32,1024]{2,1,0:T(8,128)(2,1)S(1)} async-done(((bf16[16,32,1024]{2,1,0:T(8,128)(2,1)}), bf16[16,32,1024]{2,1,0:T(8,128)(2,1)S(1)}, u32[]{:S(2)}, u32[]{:S(2)}) %all-to-all-start.1) | async-done | bytes 1048608 | tf_op jit(solution)/shard_map/all_to_all | solution.py:78
  40.7 2.3 fusion.64
  43.1 2.3 fusion.60
  47.4 5.6 %fusion.6 = f32[32,256,128]{2,1,0:T(8,128)} fusion(f32[256,32,128]{2,0,1:T(8,128)S(1)} %fusion.64, f32[256,32,128]{2,0,1:T(8,128)S(1)} %fusion.60, f32[256,128]{1,0:T(8,128)S(1)} %get-tuple-element.12, f32[256,128]{1,0:T(8,128)S(1)} %get-tuple-element.13), kind=kOutput, calls=%fused_computation.9 | convolution fusion | flops 1615036416 | bytes 12845056 | tf_op jit(solution)/shard_map/ckn,nj->ckj/dot_general | solution.py:47
  53.0 74.5 %all-gather.6.cloned.1.call-done = bf16[4096,1024]{1,0:T(8,128)(2,1)} async-done(((bf16[512,1024]{1,0:T(8,128)(2,1)}), bf16[4096,1024]{1,0:T(8,128)(2,1)}) %all-gather.6.cloned.1.call-update) | async-done | bytes 8388624 | tf_op jit(solution)/shard_map/all_gather | solution.py:81
  127.5 79.9 %all-gather.4.cloned.1.call-done = bf16[3,4096,512]{1,2,0:T(8,128)(2,1)} async-done(((bf16[3,256,512]{1,2,0:T(8,128)(2,1)}), bf16[3,4096,512]{1,2,0:T(8,128)(2,1)}) %all-gather.4.cloned.1.call-update) | async-done | bytes 12582928 | tf_op jit(solution)/shard_map/all_gather | solution.py:83
  207.3 16.7 %fusion = f32[3,512,1024]{2,1,0:T(8,128)S(1)} fusion(bf16[3,4096,512]{1,2,0:T(8,128)(2,1)} %all-gather.4.cloned.1.call-done, bf16[4096,1024]{1,0:T(8,128)(2,1)} %all-gather.6.cloned.1.call-done), kind=kOutput, calls=%fused_computation | convolution fusion | flops 12884901888 | bytes 27262976 | tf_op jit(solution)/shard_map/sic,it->sct/dot_general | solution.py:86
  224.1 2.6 copy-done.4
  227.2 2.8 collective-permute-start
  230.0 8.5 %fusion.34 = f32[32,256,128]{2,1,0:T(8,128)} fusion(f32[32,256,128]{2,1,0:T(8,128)} %fusion.6, f32[256,32,128]{2,0,1:T(8,128)} %copy-done, f32[256,32,128]{2,0,1:T(8,128)} %copy-done.2, f32[256,128]{1,0:T(8,128)S(1)} %get-tuple-element.12, f32[256,128]{1,0:T(8,128)S(1)} %get-tuple-element.13), kind=kOutput, calls=%fused_computation.39 | convolution fusion | flops 1616084992 | bytes 17039360 | tf_op jit(solution)/shard_map/ckn,nj->ckj/dot_general | solution.py:47
  239.1 9.3 %fusion.3 = f32[3,512,1024]{2,1,0:T(8,128)S(1)} fusion(f32[3,512,1023]{2,1,0:T(8,128)} %bitcast.120, f32[3,512,1]{2,1,0:T(8,128)S(1)} %copy.27, f32[3,512,1022]{2,1,0:T(8,128)} %bitcast.121, f32[3,512,2]{2,1,0:T(8,128)S(1)} %copy.28, f32[3,512,1024]{2,1,0:T(8,128)} %copy-done.4, f32[3,512]{1,0:T(4,128)S(1)} %get-tuple-element.10, ...), kind=kLoop, calls=%fused_computation.5 | loop fusion | flops 11010048 | bytes 25184256 | tf_op jit(solution)/shard_map/add | solution.py:95
  248.4 2.6 copy-done.5
  252.3 4.5 all-to-all-start
  256.9 6.8 %fusion.4 = f32[32,256,128]{2,1,0:T(8,128)S(1)} fusion(f32[256,32,128]{2,0,1:T(8,128)} %copy-done, f32[256,32,128]{2,0,1:T(8,128)} %copy-done.2, f32[256,128]{1,0:T(8,128)S(1)} %get-tuple-element.12, f32[256,128]{1,0:T(8,128)S(1)} %get-tuple-element.13), kind=kOutput, calls=%fused_computation.7 | convolution fusion | flops 1615036416 | bytes 12845056 | tf_op jit(solution)/shard_map/ckn,nj->ckj/dot_general | solution.py:50
  263.7 5.7 %fusion.37 = f32[32,256,128]{2,1,0:T(8,128)} fusion(f32[32,256,128]{2,1,0:T(8,128)S(1)} %fusion.4, f32[256,32,128]{2,0,1:T(8,128)S(1)} %copy-done.1, f32[256,32,128]{2,0,1:T(8,128)S(1)} %copy-done.3, f32[256,128]{1,0:T(8,128)S(1)} %get-tuple-element.12, f32[256,128]{1,0:T(8,128)S(1)} %get-tuple-element.13), kind=kOutput, calls=%fused_computation.40 | convolution fusion | flops 1616084992 | bytes 17039360 | tf_op jit(solution)/shard_map/ckn,nj->ckj/dot_general | solution.py:50
  269.4 3.2 all-to-all-done
  278.8 4.3 fusion.14
  283.2 5.5 %fusion.12 = f32[32,256,128]{2,1,0:T(8,128)S(1)} fusion(f32[256,32,128]{2,0,1:T(8,128)S(1)} %fusion.66, f32[256,32,128]{2,0,1:T(8,128)S(1)} %fusion.62, f32[256,128]{1,0:T(8,128)} %copy-done.6, f32[256,128]{1,0:T(8,128)} %copy-done.9), kind=kOutput, calls=%fused_computation.15 | convolution fusion | flops 1615036416 | bytes 12845056 | tf_op jit(solution)/shard_map/ckn,nj->ckj/dot_general | solution.py:50
  288.7 5.7 %fusion.28 = f32[32,256,128]{2,1,0:T(8,128)} fusion(f32[32,256,128]{2,1,0:T(8,128)S(1)} %fusion.14, f32[256,32,128]{2,0,1:T(8,128)S(1)} %fusion.66, f32[256,32,128]{2,0,1:T(8,128)S(1)} %fusion.62, f32[256,128]{1,0:T(8,128)S(1)} %copy-done.7, f32[256,128]{1,0:T(8,128)S(1)} %copy-done.10), kind=kOutput, calls=%fused_computation.37 | convolution fusion | flops 1616084992 | bytes 17039360 | tf_op jit(solution)/shard_map/ckn,nj->ckj/dot_general | solution.py:47
  294.4 8.4 %multiply_add_fusion = (f32[32,256,128]{2,1,0:T(8,128)S(1)}, f32[32,256,128]{2,1,0:T(8,128)S(1)}) fusion(f32[32,256,128]{2,1,0:T(8,128)} %fusion.34, f32[32,256,128]{2,1,0:T(8,128)} %fusion.28, f32[32,256,128]{2,1,0:T(8,128)} %fusion.37, f32[32,256,128]{2,1,0:T(8,128)S(1)} %fusion.12, f32[256,128]{1,0:T(8,128)} %copy-done.6, ...), kind=kOutput, calls=%fused_computation.31 | convolution fusion | flops 1622376448 | bytes 33816576 | tf_op jit(solution)/shard_map/ckn,nj->ckj/dot_general | solution.py:50
  302.8 3.7 fusion.86
  306.5 3.7 fusion.84
  310.1 3.7 convolution_subtract_fusion
  313.8 3.9 convolution_add_fusion
  317.7 3.3 fusion.20
  321.0 3.4 fusion.50
  325.5 19.1 %all_to_all.39 = bf16[32,16,1024]{2,0,1:T(8,128)(2,1)S(1)} all-to-all(bf16[32,16,1024]{2,0,1:T(8,128)(2,1)S(1)} %copy.35), channel_id=1, replica_groups=mesh['ctx'=16,'tp'=8] {'ctx'}, dimensions={1} | all-to-all | bytes 2097152 | tf_op jit(solution)/shard_map/all_to_all | solution.py:108
  344.6 3.4 fusion.41
  348.0 9.0 %convert_bitcast_fusion = bf16[4096,1024]{0,1:T(8,128)(2,1)} fusion(bf16[512,1024]{1,0:T(8,128)(2,1)S(1)} %fusion.41, bf16[512,4096]{1,0:T(8,128)(2,1)} %all-gather.8.cloned.1.call-done), kind=kOutput, calls=%fused_computation.2 | convolution fusion | flops 4299161600 | bytes 13631488 | tf_op jit(solution)/shard_map/cd,ct->dt/dot_general | solution.py:115
  357.0 113.9 %reduce-scatter.2.cloned.1.call-done = bf16[512,1024]{0,1:T(8,128)(2,1)} async-done(((bf16[4096,1024]{0,1:T(8,128)(2,1)}), bf16[512,1024]{0,1:T(8,128)(2,1)}) %reduce-scatter.2.cloned.1.call-update) | async-done | bytes 1048592 | tf_op jit(solution)/shard_map/reduce_scatter | solution.py:114
  (58 shorter events, 18.2 us)
Async XLA Ops:
  6.5 3.1 copy-start.12
  6.5 120.9 %all-gather.6.cloned.1.call-start = ((), (), s32[]{:S(2)}) async-start(), calls=%async_computation.5 | async-start | bytes 9437184 | tf_op jit(solution)/shard_map/all_gather | solution.py:81
  7.3 12.1 %copy-start.13 = (f32[3,512,3]{1,2,0:T(4,128)S(1)}, f32[3,512,3]{1,2,0:T(4,128)}, u32[]{:S(2)}) copy-start(f32[3,512,3]{1,2,0:T(4,128)} %param.8) | copy-start | bytes 55300
  7.3 200.1 %all-gather.4.cloned.1.call-start = ((), (), s32[]{:S(2)}) async-start(), calls=%async_computation.4 | async-start | bytes 13369344 | tf_op jit(solution)/shard_map/all_gather | solution.py:83
  10.8 28.8 %all-to-all-start.1 = ((bf16[16,32,1024]{2,1,0:T(8,128)(2,1)}), bf16[16,32,1024]{2,1,0:T(8,128)(2,1)S(1)}, u32[]{:S(2)}, u32[]{:S(2)}) async-start(bf16[16,32,1024]{2,1,0:T(8,128)(2,1)} %bitcast.11), calls=%async_computation.1 | async-start | bytes 2097152 | tf_op jit(solution)/shard_map/all_to_all | solution.py:78
  18.6 329.4 %all-gather.8.cloned.1.call-start = ((), (), s32[]{:S(2)}) async-start(), calls=%async_computation.6 | async-start | bytes 4456448 | tf_op jit(solution)/shard_map/all_gather | solution.py:113
  20.0 258.9 %copy-start.6 = (f32[256,128]{1,0:T(8,128)}, f32[256,128]{1,0:T(8,128)S(1)}, u32[]{:S(2)}) copy-start(f32[256,128]{1,0:T(8,128)S(1)} %get-tuple-element.12) | copy-start | bytes 393220
  20.0 258.9 %copy-start.9 = (f32[256,128]{1,0:T(8,128)}, f32[256,128]{1,0:T(8,128)S(1)}, u32[]{:S(2)}) copy-start(f32[256,128]{1,0:T(8,128)S(1)} %get-tuple-element.13) | copy-start | bytes 393220
  43.1 2.4 copy-start
  45.4 2.0 copy-start.2
  224.1 2.6 copy-start.4
  227.2 11.3 %collective-permute-start = (f32[3,512,2]{1,2,0:T(2,128)S(1)}, f32[3,512,2]{1,2,0:T(2,128)S(1)}, u32[]{:S(2)}, u32[]{:S(2)}) collective-permute-start(f32[3,512,2]{1,2,0:T(2,128)S(1)} %copy.26), channel_id=1, source_target_pairs={{0,8},{8,16},{16,24},{24,32},{32,40},{40,48},{48,56},{56,64},{64,7... | collective-permute-start | bytes 36872 | tf_op jit(solution)/shard_map/ppermute | solution.py:14
  248.4 2.6 copy-start.5
  252.3 20.3 %all-to-all-start = ((bf16[16,32,1024]{2,1,0:T(8,128)(2,1)}), bf16[16,32,1024]{2,1,0:T(8,128)(2,1)S(1)}, u32[]{:S(2)}, u32[]{:S(2)}) async-start(bf16[16,32,1024]{2,1,0:T(8,128)(2,1)} %bitcast.3), calls=%async_computation | async-start | bytes 2097152 | tf_op jit(solution)/shard_map/all_to_all | solution.py:100
  256.9 214.1 %reduce-scatter.2.cloned.1.call-start = ((), (), s32[]{:S(2)}) async-start(), calls=%async_computation.7 | async-start | bytes 9437184 | tf_op jit(solution)/shard_map/reduce_scatter | solution.py:114
  256.9 6.8 %copy-start.1 = (f32[256,32,128]{2,0,1:T(8,128)S(1)}, f32[256,32,128]{2,0,1:T(8,128)}, u32[]{:S(2)}) copy-start(f32[256,32,128]{2,0,1:T(8,128)} %copy-done) | copy-start | bytes 12582916
  256.9 6.8 %copy-start.3 = (f32[256,32,128]{2,0,1:T(8,128)S(1)}, f32[256,32,128]{2,0,1:T(8,128)}, u32[]{:S(2)}) copy-start(f32[256,32,128]{2,0,1:T(8,128)} %copy-done.2) | copy-start | bytes 12582916
  283.2 5.5 %copy-start.7 = (f32[256,128]{1,0:T(8,128)S(1)}, f32[256,128]{1,0:T(8,128)}, u32[]{:S(2)}) copy-start(f32[256,128]{1,0:T(8,128)} %copy-done.6) | copy-start | bytes 393220
  283.2 5.5 %copy-start.10 = (f32[256,128]{1,0:T(8,128)S(1)}, f32[256,128]{1,0:T(8,128)}, u32[]{:S(2)}) copy-start(f32[256,128]{1,0:T(8,128)} %copy-done.9) | copy-start | bytes 393220
  313.8 3.9 copy-start.8
  313.8 3.9 copy-start.11
  324.4 20.2 %copy-start.14 = (f32[512]{0:T(512)S(1)}, f32[512]{0:T(512)}, u32[]{:S(2)}) copy-start(f32[512]{0:T(512)} %param.10) | copy-start | bytes 6148
Sparse Core Ops, SparseCore 0:
  9.7 117.7 all-gather.5
  129.1 78.2 all-gather.3
  209.0 45.4 all-gather.7
  357.2 113.7 reduce-scatter.1
where the time goes:
time: 489 us; the launch traced here: 480 us
  waiting for transfers between devices  293 us (60%)
  matrix products  107 us (22%)
  blocking collectives  19.1 us (4%)
  local copies, waits for them, and re-layouts  16.7 us (3%)
  other arithmetic  15.6 us (3%)
  starting transfers between devices  15.3 us (3%)
  between operations  14 us (3%)
    reduce_scatter x1, waiting for transfers between devices, per_device(): lax.psum_scatter(jnp.einsum('cd,ct->dt', whole_out, hidden, preferred_ele...  114 us
    all_gather x1, waiting for transfers between devices, per_device(): shard_rows = lax.all_gather(in_weight, 'ctx', axis=1, tiled=True)  79.9 us
    all_gather x1, waiting for transfers between devices, per_device(): features_all = lax.all_gather(tokens, 'tp', axis=0, tiled=True)  74.5 us
    all_to_all x1, waiting for transfers between devices, per_device(): lax.all_to_all(long_filter.astype(jnp.bfloat16), 'ctx', split_axis=0, con...  19.7 us
    all_to_all x1, blocking collectives, per_device(): lax.all_to_all(long_rows, 'ctx', split_axis=1, concat_axis=0, tiled=True)  19.1 us
    dot_general x1, matrix products, per_device(): jnp.einsum('sic,it->sct', shard_rows, source, preferred_element_type=jnp....  16.7 us
    dot_general x2, matrix products, spectrum(): jnp.einsum('ckn,nj->ckj', twist_re, sin_inner, precision=HIGHEST)  14.1 us
    dot_general x2, matrix products, spectrum(): jnp.einsum('ckn,nj->ckj', twist_re, cos_inner, precision=HIGHEST)  14.1 us
  transfers between devices with their start and end apart: 7, of which 5 were waited for; matrix products, arithmetic and copies ran while one was open for 25% of the time, Pallas kernels for 0%

commit v1 on v0

v1 whole, which is shorter than its diff:
```python
import functools
import math

import jax
import jax.numpy as jnp
import numpy as np
from jax import lax
from jax.experimental import pallas as pl
from jax.experimental.pallas import tpu as pltpu
from jax.sharding import PartitionSpec as P

MESH = pl.DeviceIdType.MESH
BF16 = jnp.bfloat16
F32 = jnp.float32

RING = 4
PAIR = 2
CTX = 16
TP = 8
ROWS = 512
SLAB = 1024
WROWS = 256
OWN = 32
SIDE = 128
PART = 2
SUB = OWN // PART
HALF = ROWS // PART
BLOCK = SUB * 8

OWN_S, PAIR_S, LEFT, RIGHT, PLEFT, PRIGHT, FAR, PFAR = range(8)
COPIES = {
    "A": (0, OWN_S, PAIR_S, None, "pair"),
    "Bp": (1, OWN_S, LEFT, None, "plus"),
    "Bm": (2, OWN_S, RIGHT, None, "minus"),
    "Cp": (3, PAIR_S, PLEFT, None, "plus"),
    "Cm": (4, PAIR_S, PRIGHT, None, "minus"),
    "Dp": (5, LEFT, FAR, 0, "plus"),
    "Dm": (6, RIGHT, FAR, 1, "minus"),
    "Ep": (7, PLEFT, PFAR, 0, "plus"),
    "Em": (8, PRIGHT, PFAR, 1, "minus"),
    "AL": (3, LEFT, PLEFT, None, "pair"),
    "AR": (4, RIGHT, PRIGHT, None, "pair"),
    "AF0": (7, FAR, PFAR, 0, "pair"),
    "AF1": (8, FAR, PFAR, 1, "pair"),
}


def tables():
    i = np.arange(SIDE)
    quarter = 2 * np.pi * ((i[:, None] * (4 * i[None, :] + 1)) % (4 * SIDE)) / (4 * SIDE)
    plain = 2 * np.pi * ((i[:, None] * i[None, :]) % SIDE) / SIDE
    twist = 2 * np.pi * (((4 * i[:, None] + 1) * i[None, :]) % (4 * SIDE * SIDE)) / (4 * SIDE * SIDE)
    f1 = np.concatenate([np.cos(quarter.T), -np.sin(quarter.T)], 0)
    c, s = np.cos(plain), np.sin(plain)
    f2 = np.block([[c, -s], [s, c]])
    f3 = np.block([[c, s], [-s, c]])
    f4 = np.concatenate([np.cos(quarter), -np.sin(quarter)], 1) / (SIDE * SIDE)
    tw = np.stack([np.cos(twist), np.sin(twist)])
    return [jnp.asarray(a, BF16) for a in (f1, f2, f3, f4)] + [jnp.asarray(tw, F32)]


def rel_slot(dring, dpair):
    return 3 * dring - 7 * (dring // 3) + dpair * (1 + dring % 2)


class Gather:
    def __init__(self, devs, src, dst, got, send_sem, recv_sem):
        self.devs, self.src, self.dst, self.got = devs, src, dst, got
        self.send_sem, self.recv_sem = send_sem, recv_sem
        self.sent = []

    def send(self, *names):
        for name in names:
            i, shard, there, half, to = COPIES[name]
            copy = pltpu.make_async_remote_copy(
                src_ref=self.src(shard, half),
                dst_ref=self.dst(shard, there, half),
                send_sem=self.send_sem.at[i],
                recv_sem=self.recv_sem.at[i],
                device_id=self.devs[to],
                device_id_type=MESH,
            )
            copy.start()
            self.sent.append(copy)

    def recv(self, *names):
        for name in names:
            i, _, there, half, to = COPIES[name]
            ref = self.got(there, half)
            pltpu.make_async_copy(ref, ref, self.recv_sem.at[i]).wait()

    def finish(self):
        for copy in self.sent:
            copy.wait_send()


def dot(a, b):
    return jnp.dot(a, b, preferred_element_type=F32)


def kernel(
    tok, w, taps, filt, skip, ow, f1, f2, f3, f4, tw,
    out,
    tok_all, w_all, ow_all, hid_all, acc, w_st, ow_st, ow_send,
    fsend, frecv, gated, gsend, grecv, xf, spec, lsend, lrecv,
    halo_send, halo_recv, halo_t, rows_t, taps_t,
    local_sem, tok_ss, tok_rs, w_ss, w_rs, ow_ss, ow_rs, h_ss, h_rs, w_sib_ss, w_sib_rs, ow_sib_ss, ow_sib_rs,
    swap_sem, halo_sem, f_ss, f_rs, g_ss, g_rs, l_ss, l_rs,
):
    ctx, tp = lax.axis_index("ctx"), lax.axis_index("tp")
    y_lo, z, core = ctx // 8, (ctx // 2) % 4, ctx % 2
    y_hi, x = tp // 4, tp % 4

    def ctx_at(y, zz, c):
        return y * 8 + zz * 2 + c

    tp_devs = {
        "pair": (ctx, (1 - y_hi) * 4 + x),
        "plus": (ctx, y_hi * 4 + (x + 1) % 4),
        "minus": (ctx, y_hi * 4 + (x + 3) % 4),
    }
    ctx_devs = {
        "pair": (ctx_at(1 - y_lo, z, core), tp),
        "plus": (ctx_at(y_lo, (z + 1) % 4, core), tp),
        "minus": (ctx_at(y_lo, (z + 3) % 4, core), tp),
    }
    sibling = (ctx_at(y_lo, z, 1 - core), tp)
    swap_dev = (ctx_at(y_hi, x, core), y_lo * 4 + z)
    swap_here = (ctx // 2) == tp

    local = [
        pltpu.make_async_copy(w, w_st, local_sem.at[0]),
        pltpu.make_async_copy(ow, ow_st, local_sem.at[1]),
        pltpu.make_async_copy(filt, acc.at[0], local_sem.at[2]),
        pltpu.make_async_copy(tok, tok_all.at[pl.ds(0, ROWS)], local_sem.at[3]),
    ]
    for copy in local:
        copy.start()
    halo_recv[...] = jnp.zeros_like(halo_recv)

    barrier = pltpu.get_barrier_semaphore()
    for i in range(1, CTX):
        pl.semaphore_signal(barrier, inc=1, device_id=((ctx + i) % CTX, tp), device_id_type=MESH)
    for d in tp_devs.values():
        pl.semaphore_signal(barrier, inc=1, device_id=d, device_id_type=MESH)

    @pl.when(jnp.logical_not(swap_here))
    def _():
        pl.semaphore_signal(barrier, inc=1, device_id=swap_dev, device_id_type=MESH)
        pl.semaphore_wait(barrier, CTX + 3)

    @pl.when(swap_here)
    def _():
        pl.semaphore_wait(barrier, CTX + 2)

    def tok_src(shard, half):
        if shard == OWN_S:
            return tok
        return tok_dst(None, shard, half)

    def tok_dst(_, there, half):
        if half is None:
            return tok_all.at[pl.ds(there * ROWS, ROWS)]
        return tok_all.at[pl.ds(there * ROWS + half * HALF, HALF)]

    t_g = Gather(tp_devs, tok_src, tok_dst, lambda there, half: tok_dst(None, there, half), tok_ss, tok_rs)
    t_g.send("Bp", "Bm", "A")

    def w_slot(shard):
        dz = {OWN_S: 0, PAIR_S: 0, LEFT: 3, RIGHT: 1, PLEFT: 3, PRIGHT: 1, FAR: 2, PFAR: 2}[shard]
        dy = 1 if shard in (PAIR_S, PLEFT, PRIGHT, PFAR) else 0
        return rel_slot((z + dz + 4 - x) % 4, (y_lo + dy + y_hi) % 2)

    def w_view(shard, half, c=core):
        lanes = pl.ds(pl.multiple_of(w_slot(shard) * ROWS + c * WROWS, WROWS), WROWS)
        if half is None:
            return w_all.at[:, :, lanes]
        return w_all.at[:, pl.ds(half * HALF, HALF), lanes]

    w_g = Gather(ctx_devs, w_view, lambda shard, there, half: w_view(shard, half), w_view, w_ss, w_rs)

    def sib_copy(view, shard, ss, rs):
        return pltpu.make_async_remote_copy(
            src_ref=view(shard, None),
            dst_ref=view(shard, None),
            send_sem=ss.at[shard],
            recv_sem=rs.at[shard],
            device_id=sibling,
            device_id_type=MESH,
        )

    sib_sent = []

    def w_sib(shard):
        copy = sib_copy(w_view, shard, w_sib_ss, w_sib_rs)
        copy.start()
        sib_sent.append(copy)

    local[0].wait()
    for s in range(3):
        lanes = pl.ds(pl.multiple_of(w_slot(OWN_S) * ROWS + core * WROWS, WROWS), WROWS)
        w_all[s, :, lanes] = w_st[s].T
    w_g.send("Bp", "Bm", "A")
    w_sib(OWN_S)

    def ow_view(shard, half, c=core):
        lanes = pl.ds(pl.multiple_of(w_slot(shard) * HALF, HALF), HALF)
        rows = pl.ds(pl.multiple_of(c * WROWS, WROWS), WROWS)
        if half is None:
            return ow_all.at[:, rows, lanes]
        return ow_all.at[half, rows, lanes]

    local[1].wait()
    for h in range(PART):
        picked = jnp.concatenate([ow_st[pl.ds(d * OWN + h * SUB, SUB), :] for d in range(CTX)], axis=0)
        ow_send[h] = picked.T
    swap_lanes = pl.ds(pl.multiple_of(rel_slot((x + 4 - z) % 4, (y_hi + y_lo) % 2) * HALF, HALF), HALF)
    swap_rows = pl.ds(pl.multiple_of(core * WROWS, WROWS), WROWS)
    swap = pltpu.make_async_remote_copy(
        src_ref=ow_send,
        dst_ref=ow_all.at[:, swap_rows, swap_lanes],
        send_sem=swap_sem.at[0],
        recv_sem=swap_sem.at[1],
        device_id=swap_dev,
        device_id_type=MESH,
    )

    @pl.when(swap_here)
    def _():
        pltpu.make_async_copy(ow_send, ow_view(OWN_S, None), swap_sem.at[1]).start()

    @pl.when(jnp.logical_not(swap_here))
    def _():
        swap.start()

    rows_t[...] = jnp.zeros_like(rows_t)
    for s in range(3):
        for j in range(3):
            rows_t[3 * s + j : 3 * s + j + 1, :] = taps[s, j : j + 1, :]
    rows_t[9:10, :] = skip[...]
    taps_t[...] = rows_t[...].T

    local[2].wait()

    @pl.loop(0, ROWS // SUB)
    def _(b):
        v = acc[0, pl.ds(pl.multiple_of(b * SUB, SUB), SUB), :]
        fsend[pl.ds(pl.multiple_of(b * BLOCK, BLOCK), BLOCK), :] = v.reshape(BLOCK, SIDE).astype(BF16)

    def to_each(start):
        @pl.loop(0, CTX)
        def _(d):
            @pl.when(d != ctx)
            def _():
                start(d, True)

            @pl.when(d == ctx)
            def _():
                start(d, False)

    def filter_copy(d, remote):
        src = fsend.at[pl.ds(pl.multiple_of(d * 2 * BLOCK, 2 * BLOCK), 2 * BLOCK)]
        dst = frecv.at[ctx]
        if remote:
            return pltpu.make_async_remote_copy(
                src_ref=src, dst_ref=dst, send_sem=f_ss.at[d], recv_sem=f_rs.at[ctx],
                device_id=(d, tp), device_id_type=MESH,
            )
        return pltpu.make_async_copy(src, dst, f_rs.at[ctx])

    def part_copy(src_ref, dst_ref, ss, rs, h, d, remote):
        src, dst = src_ref.at[h, d], dst_ref.at[h, ctx]
        if remote:
            return pltpu.make_async_remote_copy(
                src_ref=src, dst_ref=dst, send_sem=ss.at[h, d], recv_sem=rs.at[h, ctx],
                device_id=(d, tp), device_id_type=MESH,
            )
        return pltpu.make_async_copy(src, dst, rs.at[h, ctx])

    w_g.recv("Bp")
    w_g.send("Dp")
    w_sib(LEFT)
    w_g.recv("Bm")
    w_g.send("Dm")
    w_sib(RIGHT)
    t_g.recv("Bp")
    t_g.send("Dp")
    t_g.recv("Bm")
    t_g.send("Dm")
    w_g.recv("A")
    w_g.send("Cp", "Cm")
    w_sib(PAIR_S)
    t_g.recv("A")
    t_g.send("Cp", "Cm")
    w_g.recv("Cp")
    w_g.send("Ep")
    w_sib(PLEFT)
    w_g.recv("Cm")
    w_g.send("Em")
    w_sib(PRIGHT)
    t_g.recv("Cp")
    t_g.send("Ep")
    t_g.recv("Cm")
    t_g.send("Em")
    to_each(lambda d, remote: filter_copy(d, remote).start())
    w_g.recv("Dp", "Dm")
    w_sib(FAR)
    w_g.recv("Ep", "Em")
    w_sib(PFAR)
    for shard in range(8):
        ref = w_view(shard, None, 1 - core)
        pltpu.make_async_copy(ref, ref, w_sib_rs.at[shard]).wait()
    local[3].wait()

    early, late = 6 * ROWS, 2 * ROWS

    @pl.loop(0, 12)
    def _(i):
        s, lanes = i // 4, pl.ds(pl.multiple_of((i % 4) * 256, 256), 256)
        acc[s, :, lanes] = dot(w_all[s, :, pl.ds(0, early)], tok_all[pl.ds(0, early), lanes])

    t_g.recv("Dp", "Dm", "Ep", "Em")

    def finish_tile(s, n):
        lanes = pl.ds(pl.multiple_of(n * 256, 256), 256)
        acc[s, :, lanes] = acc[s, :, lanes] + dot(
            w_all[s, :, pl.ds(early, late)], tok_all[pl.ds(early, late), lanes]
        )

    @pl.loop(0, 3)
    def _(s):
        finish_tile(s, 3)
        halo_send[s] = acc[s, :, pl.ds(SLAB - SIDE, SIDE)].T[SIDE - 8 :]

    halo = pltpu.make_async_remote_copy(
        src_ref=halo_send,
        dst_ref=halo_recv.at[:, pl.ds(SIDE - 8, 8)],
        send_sem=halo_sem.at[0],
        recv_sem=halo_sem.at[1],
        device_id=((ctx + 1) % CTX, tp),
        device_id_type=MESH,
    )
    halo.start()

    @pl.loop(0, 6)
    def _(i):
        finish_tile(1 + i // 3, i % 3)

    halo.wait_recv()
    for s in range(3):
        halo_t[s] = jnp.where(ctx > 0, halo_recv[s].T, 0.0)

    def short(s, r0):
        rows = pl.ds(r0, SUB)
        p = acc[s, rows, :]
        e = jnp.concatenate([halo_t[s, rows, :], p], axis=1)
        one = pltpu.roll(e, 1, 1)[:, SIDE:]
        two = pltpu.roll(e, 2, 1)[:, SIDE:]
        tap = taps_t[rows, :]
        return (
            tap[:, 3 * s : 3 * s + 1] * p
            + tap[:, 3 * s + 1 : 3 * s + 2] * one
            + tap[:, 3 * s + 2 : 3 * s + 3] * two
        )

    for h in range(PART):

        @pl.loop(0, CTX)
        def _(d):
            r0 = pl.multiple_of(d * OWN + h * SUB, SUB)
            g = (short(1, r0) * short(2, r0)).astype(BF16)
            gated[pl.ds(r0, SUB), :] = g
            gsend[h, d] = g.astype(F32).reshape(BLOCK, SIDE).astype(BF16)

            @pl.when(d != ctx)
            def _():
                part_copy(gsend, grecv, g_ss, g_rs, h, d, True).start()

            @pl.when(d == ctx)
            def _():
                part_copy(gsend, grecv, g_ss, g_rs, h, d, False).start()

    ow_g = Gather(ctx_devs, ow_view, lambda shard, there, half: ow_view(shard, half), ow_view, ow_ss, ow_rs)

    def ow_sib(shard):
        copy = sib_copy(ow_view, shard, ow_sib_ss, ow_sib_rs)
        copy.start()
        sib_sent.append(copy)

    ref = ow_view(OWN_S, None)
    pltpu.make_async_copy(ref, ref, swap_sem.at[1]).wait()
    ow_g.send("Bp", "Bm", "A")
    ow_sib(OWN_S)

    @pl.loop(0, 3)
    def _(n):
        finish_tile(0, n)

    @pl.loop(0, ROWS // SUB)
    def _(b):
        r0 = pl.multiple_of(b * SUB, SUB)
        acc[0, pl.ds(r0, SUB), :] = short(0, r0)

    def forward(c):
        pair = jnp.concatenate([xf[c].astype(BF16), xf[c + 1].astype(BF16)], axis=1)
        a = dot(f1[...], pair)
        cos, sin = tw[0], tw[1]
        turned = []
        for j in range(2):
            re, im = a[:SIDE, j * SIDE : (j + 1) * SIDE], a[SIDE:, j * SIDE : (j + 1) * SIDE]
            turned.append(jnp.concatenate([re * cos + im * sin, im * cos - re * sin], axis=1).astype(BF16))
        return dot(jnp.concatenate(turned, axis=0), f2[...])

    @pl.loop(0, CTX)
    def _(s):
        ref = frecv.at[s]
        pltpu.make_async_copy(ref, ref, f_rs.at[s]).wait()
        xf[:, pl.ds(pl.multiple_of(s * 8, 8), 8), :] = frecv[s].astype(F32).reshape(OWN, 8, SIDE)

    @pl.loop(0, OWN // 2)
    def _(i):
        spec[i] = forward(2 * i)

    def convolve(h):
        part = pl.ds(h * SUB, SUB)

        @pl.loop(0, CTX)
        def _(s):
            ref = grecv.at[h, s]
            pltpu.make_async_copy(ref, ref, g_rs.at[h, s]).wait()
            xf[part, pl.ds(pl.multiple_of(s * 8, 8), 8), :] = grecv[h, s].astype(F32).reshape(SUB, 8, SIDE)

        @pl.loop(0, SUB // 2)
        def _(i):
            c = h * SUB + 2 * i
            x_f, h_f = forward(c), spec[h * (SUB // 2) + i]
            xr, xi, hr, hi = x_f[:, :SIDE], x_f[:, SIDE:], h_f[:, :SIDE], h_f[:, SIDE:]
            prod = jnp.concatenate([xr * hr - xi * hi, xr * hi + xi * hr], axis=1).astype(BF16)
            b = dot(prod, f3[...])
            cos, sin = tw[0], tw[1]
            back = []
            for j in range(2):
                re, im = b[j * SIDE : (j + 1) * SIDE, :SIDE], b[j * SIDE : (j + 1) * SIDE, SIDE:]
                back.append(jnp.concatenate([re * cos - im * sin, im * cos + re * sin], axis=0).astype(BF16))
            y = dot(f4[...], jnp.concatenate(back, axis=1))
            xf[c] = y[:, :SIDE]
            xf[c + 1] = y[:, SIDE:]

        @pl.loop(0, CTX)
        def _(d):
            v = xf[part, pl.ds(pl.multiple_of(d * 8, 8), 8), :]
            lsend[h, d] = v.reshape(BLOCK, SIDE).astype(BF16)

            @pl.when(d != ctx)
            def _():
                part_copy(lsend, lrecv, l_ss, l_rs, h, d, True).start()

            @pl.when(d == ctx)
            def _():
                part_copy(lsend, lrecv, l_ss, l_rs, h, d, False).start()

    def hid_view(h):
        def view(shard, half):
            if half is None:
                return hid_all.at[h, pl.ds(shard * HALF, HALF)]
            return hid_all.at[h, pl.ds(shard * HALF + half * (HALF // 2), HALF // 2)]

        return view

    h_g = [
        Gather(
            tp_devs, hid_view(h), lambda shard, there, half, h=h: hid_view(h)(there, half), hid_view(h),
            h_ss.at[h], h_rs.at[h],
        )
        for h in range(PART)
    ]

    def hidden(h):
        @pl.loop(0, CTX)
        def _(d):
            ref = lrecv.at[h, d]
            pltpu.make_async_copy(ref, ref, l_rs.at[h, d]).wait()
            rows = pl.ds(pl.multiple_of(d * OWN + h * SUB, SUB), SUB)
            long_rows = lrecv[h, d].astype(F32).reshape(SUB, SLAB)
            gain = taps_t[rows, :][:, 9:10]
            v = (long_rows + gain * gated[rows, :].astype(F32)) * acc[0, rows, :]
            hid_all[h, pl.ds(pl.multiple_of(d * SUB, SUB), SUB), :] = v.astype(BF16)

    convolve(0)
    ow_g.recv("Bp")
    ow_g.send("Dp")
    ow_sib(LEFT)
    ow_g.recv("Bm")
    ow_g.send("Dm")
    ow_sib(RIGHT)
    ow_g.recv("A")
    ow_g.send("Cp", "Cm")
    ow_sib(PAIR_S)
    convolve(1)
    hidden(0)
    h_g[0].send("Bp", "Bm", "A")
    ow_g.recv("Cp")
    ow_g.send("Ep")
    ow_sib(PLEFT)
    ow_g.recv("Cm")
    ow_g.send("Em")
    ow_sib(PRIGHT)
    hidden(1)
    h_g[1].send("Bp", "Bm", "A")
    ow_g.recv("Dp", "Dm")
    ow_sib(FAR)
    ow_g.recv("Ep", "Em")
    ow_sib(PFAR)
    h_g[0].recv("Bp")
    h_g[0].send("Dp")
    h_g[0].recv("Bm")
    h_g[0].send("Dm")
    h_g[0].recv("A")
    h_g[0].send("Cp", "Cm")
    h_g[1].recv("Bp")
    h_g[1].send("Dp", "AL")
    h_g[1].recv("Bm")
    h_g[1].send("Dm", "AR")
    h_g[0].recv("Cp")
    h_g[0].send("Ep")
    h_g[0].recv("Cm")
    h_g[0].send("Em")
    h_g[1].recv("Dp")
    h_g[1].send("AF0")
    h_g[1].recv("Dm")
    h_g[1].send("AF1")
    for shard in range(8):
        ref = ow_view(shard, None, 1 - core)
        pltpu.make_async_copy(ref, ref, ow_sib_rs.at[shard]).wait()

    def outward(h, k0, k1, first, last):
        @pl.loop(0, 4)
        def _(n):
            lanes = pl.ds(pl.multiple_of(n * 256, 256), 256)
            v = dot(ow_all[h, :, pl.ds(k0, k1 - k0)], hid_all[h, pl.ds(k0, k1 - k0), lanes])
            if not first:
                v = v + acc[1, :, lanes]
            if last:
                out[:, lanes] = v.astype(BF16)
            else:
                acc[1, :, lanes] = v

    outward(0, 0, 6 * HALF, True, False)
    h_g[0].recv("Dp", "Dm", "Ep", "Em")
    outward(0, 6 * HALF, 8 * HALF, False, False)
    h_g[1].recv("A", "AL", "AR")
    outward(1, 0, 6 * HALF, False, False)
    h_g[1].recv("AF0", "AF1")
    outward(1, 6 * HALF, 8 * HALF, False, True)

    for gather in (t_g, w_g, ow_g, *h_g):
        gather.finish()
    for copy in sib_sent:
        copy.wait_send()

    @pl.when(jnp.logical_not(swap_here))
    def _():
        swap.wait_send()

    halo.wait_send()

    @pl.loop(0, CTX)
    def _(d):
        @pl.when(d != ctx)
        def _():
            filter_copy(d, True).wait_send()
            for h in range(PART):
                part_copy(gsend, grecv, g_ss, g_rs, h, d, True).wait_send()
                part_copy(lsend, lrecv, l_ss, l_rs, h, d, True).wait_send()


def per_device(tokens, in_weight, short_taps, long_filter, skip_gain, out_weight):
    hbm = pl.BlockSpec(memory_space=pl.ANY)
    vmem = pl.BlockSpec(memory_space=pltpu.VMEM)
    dma = pltpu.SemaphoreType.DMA
    return pl.pallas_call(
        kernel,
        out_shape=jax.ShapeDtypeStruct((ROWS, SLAB), BF16),
        in_specs=[hbm, hbm, vmem, hbm, vmem, hbm, vmem, vmem, vmem, vmem, vmem],
        out_specs=vmem,
        scratch_shapes=[
            pltpu.VMEM((TP * ROWS, SLAB), BF16),
            pltpu.VMEM((3, ROWS, TP * ROWS), BF16),
            pltpu.VMEM((PART, ROWS, TP * HALF), BF16),
            pltpu.VMEM((PART, TP * HALF, SLAB), BF16),
            pltpu.VMEM((3, ROWS, SLAB), F32),
            pltpu.VMEM((3, WROWS, ROWS), BF16),
            pltpu.VMEM((ROWS, WROWS), BF16),
            pltpu.VMEM((PART, WROWS, HALF), BF16),
            pltpu.VMEM((ROWS * 8, SIDE), BF16),
            pltpu.VMEM((CTX, 2 * BLOCK, SIDE), BF16),
            pltpu.VMEM((ROWS, SLAB), BF16),
            pltpu.VMEM((PART, CTX, BLOCK, SIDE), BF16),
            pltpu.VMEM((PART, CTX, BLOCK, SIDE), BF16),
            pltpu.VMEM((OWN, SIDE, SIDE), F32),
            pltpu.VMEM((OWN // 2, 2 * SIDE, 2 * SIDE), F32),
            pltpu.VMEM((PART, CTX, BLOCK, SIDE), BF16),
            pltpu.VMEM((PART, CTX, BLOCK, SIDE), BF16),
            pltpu.VMEM((3, 8, ROWS), F32),
            pltpu.VMEM((3, SIDE, ROWS), F32),
            pltpu.VMEM((3, ROWS, SIDE), F32),
            pltpu.VMEM((SIDE, ROWS), F32),
            pltpu.VMEM((ROWS, SIDE), F32),
            dma((4,)),
            dma((9,)), dma((9,)),
            dma((9,)), dma((9,)),
            dma((9,)), dma((9,)),
            dma((PART, 9)), dma((PART, 9)),
            dma((8,)), dma((8,)),
            dma((8,)), dma((8,)),
            dma((2,)),
            dma((2,)),
            dma((CTX,)), dma((CTX,)),
            dma((PART, CTX)), dma((PART, CTX)),
            dma((PART, CTX)), dma((PART, CTX)),
        ],
        compiler_params=pltpu.CompilerParams(
            collective_id=0, has_side_effects=True, vmem_limit_bytes=62 * 2**20
        ),
        cost_estimate=pl.CostEstimate(
            flops=2 * (3 * ROWS * TP * ROWS * SLAB + TP * ROWS * ROWS * SLAB) + 2_400_000_000,
            bytes_accessed=8 * 2**20,
            transcendentals=0,
        ),
        name="hyena",
    )(
        tokens,
        in_weight,
        jnp.swapaxes(short_taps, 1, 2),
        long_filter,
        skip_gain.reshape(1, ROWS),
        out_weight,
        *tables(),
    )


def solution(mesh):
    placed = (
        P("tp", "ctx"),
        P(None, "ctx", "tp"),
        P(None, "tp", None),
        P("tp", "ctx"),
        P("tp"),
        P("tp", "ctx"),
    )
    return jax.shard_map(
        per_device, mesh=mesh, in_specs=placed, out_specs=P("tp", "ctx"), check_vma=False
    )
```

time: 489 us -> 206 us (0.42); the launches traced: 480 us -> 205 us
  waiting for transfers between devices: 293 us -> 0 us
  Pallas kernels: 0 us -> 203 us
  matrix products: 107 us -> 0 us
  blocking collectives: 19.1 us -> 0 us
  other arithmetic: 15.6 us -> 0 us
  starting transfers between devices: 15.3 us -> 0 us
  local copies, waits for them, and re-layouts: 16.7 us -> 2.26 us
  between operations: 14 us -> 0.01 us
    pallas_call x0 -> x1, Pallas kernels: none -> 203 us  [per_device(): pl.pallas_call(kernel, out_shape=jax.ShapeDtypeStruct((ROWS, SLAB), BF16)...]
    all_gather x3 -> x0, waiting for transfers between devices: 154 us -> none  [the longest x1 79.9 us: per_device(): shard_rows = lax.all_gather(in_weight, 'ctx', axis=1, tiled=True)]
    reduce_scatter x1 -> x0, waiting for transfers between devices: 114 us -> none  [per_device(): lax.psum_scatter(jnp.einsum('cd,ct->dt', whole_out, hidden, preferred_ele...]
    dot_general x20 -> x0, matrix products: 107 us -> none  [the longest x1 16.7 us: per_device(): jnp.einsum('sic,it->sct', shard_rows, source, preferred_element_type=jnp....]
    all_to_all x2 -> x0, waiting for transfers between devices: 22.9 us -> none  [the longest x1 19.7 us: per_device(): lax.all_to_all(long_filter.astype(jnp.bfloat16), 'ctx', split_axis=0, con...]
    all_to_all x1 -> x0, blocking collectives: 19.1 us -> none  [per_device(): lax.all_to_all(long_rows, 'ctx', split_axis=1, concat_axis=0, tiled=True)]
    all_to_all x2 -> x0, starting transfers between devices: 12.4 us -> none  [the longest x1 7.84 us: per_device(): lax.all_to_all(long_filter.astype(jnp.bfloat16), 'ctx', split_axis=0, con...]
    add x1 -> x0, other arithmetic: 9.28 us -> none  [per_device(): short_taps[:, :, 0:1] * projected + short_taps[:, :, 1:2] * prev_one]
  transfers between devices with their start and end apart: 7 -> 0, of which waited for: 5 -> 0; matrix products, arithmetic and copies ran while one was open for 25% -> 0% of each run, Pallas kernels for 0% -> 0%
where the time goes in v1:
time: 206 us; the launch traced here: 205 us
  Pallas kernels  203 us (99%)
  local copies, waits for them, and re-layouts  2.26 us (1%)
    pallas_call x1, Pallas kernels, per_device(): pl.pallas_call(kernel, out_shape=jax.ShapeDtypeStruct((ROWS, SLAB), BF16)...  203 us

profile of v1, /device:TPU:1, one launch (start us, length us, event | category | flops | bytes accessed | tf_op | source)
XLA Modules:
  0.0 205.4 jit_solution(176967632192927552)
XLA Ops:
  0.0 203.1 %hyena.1 = bf16[512,1024]{1,0:T(8,128)(2,1)} custom-call(bf16[512,1024]{1,0:T(8,128)(2,1)} %tok.1, bf16[3,256,512]{2,1,0:T(8,128)(2,1)} %w.1, f32[3,3,512]{2,1,0:T(4,128)} %bitcast.2, f32[512,1024]{1,0:T(8,128)} %filt.1, f32[1,512]{1,0:T(1,128)} %bitcast.3, bf16[512,256]{1,0:T(8,128)(2,1)} %ow.1, bf16[256,128]{1,0:T(8,128)(2,1)} %constant.10.clone.f1, ...), custom_call_target="tpu_custom_call" | custom-call | flops 19579869184 | bytes 8388608 | tf_op jit(solution)/shard_map/hyena/pallas_call | solution.py:581
  203.1 2.3 %copy.13 = bf16[512,1024]{1,0:T(8,128)(2,1)} copy(bf16[512,1024]{1,0:T(8,128)(2,1)} %hyena.1) | data formatting | bytes 2097152

commit v2 on v1

--- a/solution.py
+++ b/solution.py
@@ -25,6 +25,7 @@
 PART = 2
 SUB = OWN // PART
 HALF = ROWS // PART
+PIECES = ((0, 0, HALF), (1, 0, 64), (1, 64, HALF - 64))
 BLOCK = SUB * 8
 
 OWN_S, PAIR_S, LEFT, RIGHT, PLEFT, PRIGHT, FAR, PFAR = range(8)
@@ -101,7 +102,7 @@
 def kernel(
     tok, w, taps, filt, skip, ow, f1, f2, f3, f4, tw,
     out,
-    tok_all, w_all, ow_all, hid_all, acc, w_st, ow_st, ow_send,
+    tok_all, w_all, ow_all, hid_all, acc, w_st, ow_st, ow_send, ow_held,
     fsend, frecv, gated, gsend, grecv, xf, spec, lsend, lrecv,
     halo_send, halo_recv, halo_t, rows_t, taps_t,
     local_sem, tok_ss, tok_rs, w_ss, w_rs, ow_ss, ow_rs, h_ss, h_rs, w_sib_ss, w_sib_rs, ow_sib_ss, ow_sib_rs,
@@ -125,8 +126,10 @@
         "minus": (ctx_at(y_lo, (z + 3) % 4, core), tp),
     }
     sibling = (ctx_at(y_lo, z, 1 - core), tp)
-    swap_dev = (ctx_at(y_hi, x, core), y_lo * 4 + z)
-    swap_here = (ctx // 2) == tp
+    cross_dev = (ctx_at(y_hi, z, core), y_lo * 4 + x)
+    cross_away = y_hi != y_lo
+    swap_dev = (ctx_at(y_lo, x, core), y_hi * 4 + z)
+    swap_away = x != z
 
     local = [
         pltpu.make_async_copy(w, w_st, local_sem.at[0]),
@@ -144,40 +147,53 @@
     for d in tp_devs.values():
         pl.semaphore_signal(barrier, inc=1, device_id=d, device_id_type=MESH)
 
-    @pl.when(jnp.logical_not(swap_here))
+    @pl.when(cross_away)
+    def _():
+        pl.semaphore_signal(barrier, inc=1, device_id=cross_dev, device_id_type=MESH)
+
+    @pl.when(swap_away)
     def _():
         pl.semaphore_signal(barrier, inc=1, device_id=swap_dev, device_id_type=MESH)
-        pl.semaphore_wait(barrier, CTX + 3)
-
-    @pl.when(swap_here)
-    def _():
-        pl.semaphore_wait(barrier, CTX + 2)
-
-    def tok_src(shard, half):
-        if shard == OWN_S:
-            return tok
-        return tok_dst(None, shard, half)
-
-    def tok_dst(_, there, half):
-        if half is None:
-            return tok_all.at[pl.ds(there * ROWS, ROWS)]
-        return tok_all.at[pl.ds(there * ROWS + half * HALF, HALF)]
-
-    t_g = Gather(tp_devs, tok_src, tok_dst, lambda there, half: tok_dst(None, there, half), tok_ss, tok_rs)
-    t_g.send("Bp", "Bm", "A")
+
+    pl.semaphore_wait(barrier, CTX - 1 + 3 + cross_away.astype(jnp.int32) + swap_away.astype(jnp.int32))
+
+    def tok_gather(k):
+        def rows(shard, half):
+            if half is None:
+                return pl.ds(shard * ROWS + k * HALF, HALF)
+            return pl.ds(shard * ROWS + k * HALF + half * (HALF // 2), HALF // 2)
+
+        def src(shard, half):
+            return (tok if shard == OWN_S else tok_all).at[rows(shard, half)]
+
+        return Gather(
+            tp_devs, src, lambda shard, there, half: tok_all.at[rows(there, half)],
+            lambda there, half: tok_all.at[rows(there, half)], tok_ss.at[k], tok_rs.at[k],
+        )
+
+    t_g = [tok_gather(k) for k in range(2)]
+    t_g[0].send("Bp", "Bm")
 
     def w_slot(shard):
         dz = {OWN_S: 0, PAIR_S: 0, LEFT: 3, RIGHT: 1, PLEFT: 3, PRIGHT: 1, FAR: 2, PFAR: 2}[shard]
         dy = 1 if shard in (PAIR_S, PLEFT, PRIGHT, PFAR) else 0
         return rel_slot((z + dz + 4 - x) % 4, (y_lo + dy + y_hi) % 2)
 
+    def w_lanes(shard, c):
+        return pl.ds(pl.multiple_of(w_slot(shard) * ROWS + c * WROWS, WROWS), WROWS)
+
     def w_view(shard, half, c=core):
-        lanes = pl.ds(pl.multiple_of(w_slot(shard) * ROWS + c * WROWS, WROWS), WROWS)
-        if half is None:
-            return w_all.at[:, :, lanes]
-        return w_all.at[:, pl.ds(half * HALF, HALF), lanes]
-
-    w_g = Gather(ctx_devs, w_view, lambda shard, there, half: w_view(shard, half), w_view, w_ss, w_rs)
+        return w_all.at[:, :, w_lanes(shard, c)]
+
+    def w_gather(k):
+        def view(shard, half):
+            if half is None:
+                return w_all.at[:, pl.ds(k * HALF, HALF), w_lanes(shard, core)]
+            return w_all.at[:, pl.ds(k * HALF + half * (HALF // 2), HALF // 2), w_lanes(shard, core)]
+
+        return Gather(ctx_devs, view, lambda shard, there, half: view(shard, half), view, w_ss.at[k], w_rs.at[k])
+
+    w_g = [w_gather(k) for k in range(2)]
 
     def sib_copy(view, shard, ss, rs):
         return pltpu.make_async_remote_copy(
@@ -198,9 +214,9 @@
 
     local[0].wait()
     for s in range(3):
-        lanes = pl.ds(pl.multiple_of(w_slot(OWN_S) * ROWS + core * WROWS, WROWS), WROWS)
-        w_all[s, :, lanes] = w_st[s].T
-    w_g.send("Bp", "Bm", "A")
+        w_all[s, :, w_lanes(OWN_S, core)] = w_st[s].T
+    w_g[0].send("A", "Bp", "Bm")
+    w_g[1].send("A")
     w_sib(OWN_S)
 
     def ow_view(shard, half, c=core):
@@ -214,24 +230,25 @@
     for h in range(PART):
         picked = jnp.concatenate([ow_st[pl.ds(d * OWN + h * SUB, SUB), :] for d in range(CTX)], axis=0)
         ow_send[h] = picked.T
+    cross = pltpu.make_async_remote_copy(
+        src_ref=ow_send,
+        dst_ref=ow_held,
+        send_sem=swap_sem.at[0],
+        recv_sem=swap_sem.at[1],
+        device_id=cross_dev,
+        device_id_type=MESH,
+    )
+
     swap_lanes = pl.ds(pl.multiple_of(rel_slot((x + 4 - z) % 4, (y_hi + y_lo) % 2) * HALF, HALF), HALF)
     swap_rows = pl.ds(pl.multiple_of(core * WROWS, WROWS), WROWS)
     swap = pltpu.make_async_remote_copy(
-        src_ref=ow_send,
+        src_ref=ow_held,
         dst_ref=ow_all.at[:, swap_rows, swap_lanes],
-        send_sem=swap_sem.at[0],
-        recv_sem=swap_sem.at[1],
+        send_sem=swap_sem.at[2],
+        recv_sem=swap_sem.at[3],
         device_id=swap_dev,
         device_id_type=MESH,
     )
-
-    @pl.when(swap_here)
-    def _():
-        pltpu.make_async_copy(ow_send, ow_view(OWN_S, None), swap_sem.at[1]).start()
-
-    @pl.when(jnp.logical_not(swap_here))
-    def _():
-        swap.start()
 
     rows_t[...] = jnp.zeros_like(rows_t)
     for s in range(3):
@@ -277,36 +294,55 @@
             )
         return pltpu.make_async_copy(src, dst, rs.at[h, ctx])
 
-    w_g.recv("Bp")
-    w_g.send("Dp")
+    w_g[0].recv("Bp", "Bm")
+    w_g[1].send("Bp", "Bm")
+    w_g[0].send("Dp", "Dm")
+    t_g[0].send("A")
+    t_g[1].send("Bp", "Bm")
+    t_g[0].recv("Bp", "Bm")
+    t_g[0].send("Dp", "Dm")
+    t_g[1].send("A")
+    w_g[1].recv("Bp", "Bm")
+    w_g[1].send("Dp", "Dm")
     w_sib(LEFT)
-    w_g.recv("Bm")
-    w_g.send("Dm")
     w_sib(RIGHT)
-    t_g.recv("Bp")
-    t_g.send("Dp")
-    t_g.recv("Bm")
-    t_g.send("Dm")
-    w_g.recv("A")
-    w_g.send("Cp", "Cm")
+    w_g[0].recv("A")
+    w_g[0].send("Cp", "Cm")
+    w_g[1].recv("A")
+    w_g[1].send("Cp", "Cm")
     w_sib(PAIR_S)
-    t_g.recv("A")
-    t_g.send("Cp", "Cm")
-    w_g.recv("Cp")
-    w_g.send("Ep")
+    t_g[0].recv("A")
+    t_g[0].send("Cp", "Cm")
+    t_g[1].recv("Bp", "Bm")
+    t_g[1].send("Dp", "Dm")
+    w_g[0].recv("Cp", "Cm")
+    w_g[0].send("Ep", "Em")
+    t_g[1].recv("A")
+    t_g[1].send("Cp", "Cm")
+
+    @pl.when(cross_away)
+    def _():
+        cross.start()
+
+    @pl.when(jnp.logical_not(cross_away))
+    def _():
+        pltpu.make_async_copy(ow_send, ow_held, swap_sem.at[1]).start()
+
+    w_g[1].recv("Cp", "Cm")
+    w_g[1].send("Ep", "Em")
     w_sib(PLEFT)
-    w_g.recv("Cm")
-    w_g.send("Em")
     w_sib(PRIGHT)
-    t_g.recv("Cp")
-    t_g.send("Ep")
-    t_g.recv("Cm")
-    t_g.send("Em")
+    for g in w_g:
+        g.recv("Dp", "Dm")
+    w_sib(FAR)
+    t_g[0].recv("Cp", "Cm")
+    t_g[0].send("Ep", "Em")
+    for g in w_g:
+        g.recv("Ep", "Em")
+    w_sib(PFAR)
     to_each(lambda d, remote: filter_copy(d, remote).start())
-    w_g.recv("Dp", "Dm")
-    w_sib(FAR)
-    w_g.recv("Ep", "Em")
-    w_sib(PFAR)
+    t_g[1].recv("Cp", "Cm")
+    t_g[1].send("Ep", "Em")
     for shard in range(8):
         ref = w_view(shard, None, 1 - core)
         pltpu.make_async_copy(ref, ref, w_sib_rs.at[shard]).wait()
@@ -319,7 +355,38 @@
         s, lanes = i // 4, pl.ds(pl.multiple_of((i % 4) * 256, 256), 256)
         acc[s, :, lanes] = dot(w_all[s, :, pl.ds(0, early)], tok_all[pl.ds(0, early), lanes])
 
-    t_g.recv("Dp", "Dm", "Ep", "Em")
+    def forward(c):
+        pair = jnp.concatenate([xf[c].astype(BF16), xf[c + 1].astype(BF16)], axis=1)
+        a = dot(f1[...], pair)
+        cos, sin = tw[0], tw[1]
+        turned = []
+        for j in range(2):
+            re, im = a[:SIDE, j * SIDE : (j + 1) * SIDE], a[SIDE:, j * SIDE : (j + 1) * SIDE]
+            turned.append(jnp.concatenate([re * cos + im * sin, im * cos - re * sin], axis=1).astype(BF16))
+        return dot(jnp.concatenate(turned, axis=0), f2[...])
+
+    @pl.loop(0, CTX)
+    def _(s):
+        ref = frecv.at[s]
+        pltpu.make_async_copy(ref, ref, f_rs.at[s]).wait()
+        xf[:, pl.ds(pl.multiple_of(s * 8, 8), 8), :] = frecv[s].astype(F32).reshape(OWN, 8, SIDE)
+
+    @pl.loop(0, OWN // 2, unroll=4)
+    def _(i):
+        spec[i] = forward(2 * i)
+
+    for g in t_g:
+        g.recv("Dp", "Dm", "Ep", "Em")
+
+    pltpu.make_async_copy(ow_held, ow_held, swap_sem.at[1]).wait()
+
+    @pl.when(swap_away)
+    def _():
+        swap.start()
+
+    @pl.when(jnp.logical_not(swap_away))
+    def _():
+        pltpu.make_async_copy(ow_held, ow_view(OWN_S, None), swap_sem.at[3]).start()
 
     def finish_tile(s, n):
         lanes = pl.ds(pl.multiple_of(n * 256, 256), 256)
@@ -387,11 +454,6 @@
         copy.start()
         sib_sent.append(copy)
 
-    ref = ow_view(OWN_S, None)
-    pltpu.make_async_copy(ref, ref, swap_sem.at[1]).wait()
-    ow_g.send("Bp", "Bm", "A")
-    ow_sib(OWN_S)
-
     @pl.loop(0, 3)
     def _(n):
         finish_tile(0, n)
@@ -401,27 +463,7 @@
         r0 = pl.multiple_of(b * SUB, SUB)
         acc[0, pl.ds(r0, SUB), :] = short(0, r0)
 
-    def forward(c):
-        pair = jnp.concatenate([xf[c].astype(BF16), xf[c + 1].astype(BF16)], axis=1)
-        a = dot(f1[...], pair)
-        cos, sin = tw[0], tw[1]
-        turned = []
-        for j in range(2):
-            re, im = a[:SIDE, j * SIDE : (j + 1) * SIDE], a[SIDE:, j * SIDE : (j + 1) * SIDE]
-            turned.append(jnp.concatenate([re * cos + im * sin, im * cos - re * sin], axis=1).astype(BF16))
-        return dot(jnp.concatenate(turned, axis=0), f2[...])
-
-    @pl.loop(0, CTX)
-    def _(s):
-        ref = frecv.at[s]
-        pltpu.make_async_copy(ref, ref, f_rs.at[s]).wait()
-        xf[:, pl.ds(pl.multiple_of(s * 8, 8), 8), :] = frecv[s].astype(F32).reshape(OWN, 8, SIDE)
-
-    @pl.loop(0, OWN // 2)
-    def _(i):
-        spec[i] = forward(2 * i)
-
-    def convolve(h):
+    def take(h):
         part = pl.ds(h * SUB, SUB)
 
         @pl.loop(0, CTX)
@@ -430,7 +472,10 @@
             pltpu.make_async_copy(ref, ref, g_rs.at[h, s]).wait()
             xf[part, pl.ds(pl.multiple_of(s * 8, 8), 8), :] = grecv[h, s].astype(F32).reshape(SUB, 8, SIDE)
 
-        @pl.loop(0, SUB // 2)
+    def convolve(h):
+        part = pl.ds(h * SUB, SUB)
+
+        @pl.loop(0, SUB // 2, unroll=4)
         def _(i):
             c = h * SUB + 2 * i
             x_f, h_f = forward(c), spec[h * (SUB // 2) + i]
@@ -459,21 +504,19 @@
             def _():
                 part_copy(lsend, lrecv, l_ss, l_rs, h, d, False).start()
 
-    def hid_view(h):
+    def hid_gather(i):
+        h, first, count = PIECES[i]
+
         def view(shard, half):
             if half is None:
-                return hid_all.at[h, pl.ds(shard * HALF, HALF)]
-            return hid_all.at[h, pl.ds(shard * HALF + half * (HALF // 2), HALF // 2)]
-
-        return view
-
-    h_g = [
-        Gather(
-            tp_devs, hid_view(h), lambda shard, there, half, h=h: hid_view(h)(there, half), hid_view(h),
-            h_ss.at[h], h_rs.at[h],
+                return hid_all.at[h, pl.ds(shard * HALF + first, count)]
+            return hid_all.at[h, pl.ds(shard * HALF + first + half * (count // 2), count // 2)]
+
+        return Gather(
+            tp_devs, view, lambda shard, there, half: view(there, half), view, h_ss.at[i], h_rs.at[i]
         )
-        for h in range(PART)
-    ]
+
+    h_g = [hid_gather(i) for i in range(len(PIECES))]
 
     def hidden(h):
         @pl.loop(0, CTX)
@@ -486,49 +529,54 @@
             v = (long_rows + gain * gated[rows, :].astype(F32)) * acc[0, rows, :]
             hid_all[h, pl.ds(pl.multiple_of(d * SUB, SUB), SUB), :] = v.astype(BF16)
 
+    take(0)
     convolve(0)
-    ow_g.recv("Bp")
-    ow_g.send("Dp")
+    ref = ow_view(OWN_S, None)
+    pltpu.make_async_copy(ref, ref, swap_sem.at[3]).wait()
+    take(1)
+    ow_g.send("A", "Bp", "Bm")
+    ow_sib(OWN_S)
+    convolve(1)
+    hidden(0)
+    h_g[0].send("A", "Bp", "Bm")
+    ow_g.recv("Bp", "Bm")
+    ow_g.send("Dp", "Dm")
     ow_sib(LEFT)
-    ow_g.recv("Bm")
-    ow_g.send("Dm")
     ow_sib(RIGHT)
     ow_g.recv("A")
     ow_g.send("Cp", "Cm")
     ow_sib(PAIR_S)
-    convolve(1)
-    hidden(0)
-    h_g[0].send("Bp", "Bm", "A")
-    ow_g.recv("Cp")
-    ow_g.send("Ep")
+    hidden(1)
+    h_g[2].send("Bp", "Bm", "A")
+    h_g[1].send("A", "Bp", "Bm")
+    ow_g.recv("Cp", "Cm")
+    ow_g.send("Ep", "Em")
     ow_sib(PLEFT)
-    ow_g.recv("Cm")
-    ow_g.send("Em")
     ow_sib(PRIGHT)
-    hidden(1)
-    h_g[1].send("Bp", "Bm", "A")
+    h_g[0].recv("Bp", "Bm")
+    h_g[0].send("Dp", "Dm")
+    h_g[0].recv("A")
+    h_g[0].send("Cp", "Cm")
     ow_g.recv("Dp", "Dm")
     ow_sib(FAR)
     ow_g.recv("Ep", "Em")
     ow_sib(PFAR)
-    h_g[0].recv("Bp")
-    h_g[0].send("Dp")
-    h_g[0].recv("Bm")
-    h_g[0].send("Dm")
-    h_g[0].recv("A")
-    h_g[0].send("Cp", "Cm")
-    h_g[1].recv("Bp")
-    h_g[1].send("Dp", "AL")
-    h_g[1].recv("Bm")
-    h_g[1].send("Dm", "AR")
-    h_g[0].recv("Cp")
-    h_g[0].send("Ep")
-    h_g[0].recv("Cm")
-    h_g[0].send("Em")
-    h_g[1].recv("Dp")
-    h_g[1].send("AF0")
-    h_g[1].recv("Dm")
-    h_g[1].send("AF1")
+    h_g[2].recv("Bp")
+    h_g[2].send("Dp", "AL")
+    h_g[2].recv("Bm")
+    h_g[2].send("Dm", "AR")
+    h_g[1].recv("Bp", "Bm")
+    h_g[1].send("Dp", "Dm")
+    h_g[1].recv("A")
+    h_g[1].send("Cp", "Cm")
+    h_g[0].recv("Cp", "Cm")
+    h_g[0].send("Ep", "Em")
+    h_g[2].recv("Dp")
+    h_g[2].send("AF0")
+    h_g[2].recv("Dm")
+    h_g[2].send("AF1")
+    h_g[1].recv("Cp", "Cm")
+    h_g[1].send("Ep", "Em")
     for shard in range(8):
         ref = ow_view(shard, None, 1 - core)
         pltpu.make_async_copy(ref, ref, ow_sib_rs.at[shard]).wait()
@@ -548,17 +596,22 @@
     outward(0, 0, 6 * HALF, True, False)
     h_g[0].recv("Dp", "Dm", "Ep", "Em")
     outward(0, 6 * HALF, 8 * HALF, False, False)
-    h_g[1].recv("A", "AL", "AR")
+    h_g[2].recv("A", "AL", "AR")
     outward(1, 0, 6 * HALF, False, False)
-    h_g[1].recv("AF0", "AF1")
+    h_g[1].recv("Dp", "Dm", "Ep", "Em")
+    h_g[2].recv("AF0", "AF1")
     outward(1, 6 * HALF, 8 * HALF, False, True)
 
-    for gather in (t_g, w_g, ow_g, *h_g):
+    for gather in (*t_g, *w_g, ow_g, *h_g):
         gather.finish()
     for copy in sib_sent:
         copy.wait_send()
 
-    @pl.when(jnp.logical_not(swap_here))
+    @pl.when(cross_away)
+    def _():
+        cross.wait_send()
+
+    @pl.when(swap_away)
     def _():
         swap.wait_send()
 
@@ -592,6 +645,7 @@
             pltpu.VMEM((3, WROWS, ROWS), BF16),
             pltpu.VMEM((ROWS, WROWS), BF16),
             pltpu.VMEM((PART, WROWS, HALF), BF16),
+            pltpu.VMEM((PART, WROWS, HALF), BF16),
             pltpu.VMEM((ROWS * 8, SIDE), BF16),
             pltpu.VMEM((CTX, 2 * BLOCK, SIDE), BF16),
             pltpu.VMEM((ROWS, SLAB), BF16),
@@ -607,13 +661,13 @@
             pltpu.VMEM((SIDE, ROWS), F32),
             pltpu.VMEM((ROWS, SIDE), F32),
             dma((4,)),
+            dma((2, 9)), dma((2, 9)),
+            dma((2, 9)), dma((2, 9)),
             dma((9,)), dma((9,)),
-            dma((9,)), dma((9,)),
-            dma((9,)), dma((9,)),
-            dma((PART, 9)), dma((PART, 9)),
+            dma((3, 9)), dma((3, 9)),
             dma((8,)), dma((8,)),
             dma((8,)), dma((8,)),
-            dma((2,)),
+            dma((4,)),
             dma((2,)),
             dma((CTX,)), dma((CTX,)),
             dma((PART, CTX)), dma((PART, CTX)),

time: 206 us -> 189 us (0.917)
  the two profiles are of different devices: /device:TPU:1 before, /device:TPU:106 now
where the time goes in v2:
time: 189 us
  Pallas kernels  187 us (99%)
  local copies, waits for them, and re-layouts  2.26 us (1%)
    pallas_call x1, Pallas kernels, per_device(): pl.pallas_call(kernel, out_shape=jax.ShapeDtypeStruct((ROWS, SLAB), BF16)...  187 us

profile of v2, /device:TPU:106, one launch (start us, length us, event | category | flops | bytes accessed | tf_op | source)
XLA Modules:
  0.0 189.2 jit_solution(16345320599179640241)
XLA Ops:
  0.0 186.9 %hyena.1 = bf16[512,1024]{1,0:T(8,128)(2,1)} custom-call(bf16[512,1024]{1,0:T(8,128)(2,1)} %tok.1, bf16[3,256,512]{2,1,0:T(8,128)(2,1)} %w.1, f32[3,3,512]{2,1,0:T(4,128)} %bitcast.2, f32[512,1024]{1,0:T(8,128)} %filt.1, f32[1,512]{1,0:T(1,128)} %bitcast.3, bf16[512,256]{1,0:T(8,128)(2,1)} %ow.1, bf16[256,128]{1,0:T(8,128)(2,1)} %constant.10.clone.f1, ...), custom_call_target="tpu_custom_call" | custom-call | flops 19579869184 | bytes 8388608 | tf_op jit(solution)/shard_map/hyena/pallas_call | solution.py:634
  186.9 2.3 %copy.13 = bf16[512,1024]{1,0:T(8,128)(2,1)} copy(bf16[512,1024]{1,0:T(8,128)(2,1)} %hyena.1) | data formatting | bytes 2097152

commit v3 on v2

--- a/solution.py
+++ b/solution.py
@@ -126,10 +126,14 @@
         "minus": (ctx_at(y_lo, (z + 3) % 4, core), tp),
     }
     sibling = (ctx_at(y_lo, z, 1 - core), tp)
-    cross_dev = (ctx_at(y_hi, z, core), y_lo * 4 + x)
-    cross_away = y_hi != y_lo
-    swap_dev = (ctx_at(y_lo, x, core), y_hi * 4 + z)
-    swap_away = x != z
+    cross_dev = (ctx_at(y_hi, (z + x) % 4, core), y_lo * 4 + x)
+    cross_from = (ctx_at(y_hi, (z + 4 - x) % 4, core), y_lo * 4 + x)
+    cross_group = y_hi != y_lo
+    cross_away = jnp.logical_or(cross_group, x != 0)
+    swap_dev = (ctx, y_hi * 4 + (z + 4 - x) % 4)
+    swap_by = (z + 8 - 2 * x) % 4
+    swap_away = swap_by != 0
+    swap_far = swap_by == 2
 
     local = [
         pltpu.make_async_copy(w, w_st, local_sem.at[0]),
@@ -147,15 +151,15 @@
     for d in tp_devs.values():
         pl.semaphore_signal(barrier, inc=1, device_id=d, device_id_type=MESH)
 
-    @pl.when(cross_away)
+    @pl.when(cross_group)
     def _():
-        pl.semaphore_signal(barrier, inc=1, device_id=cross_dev, device_id_type=MESH)
-
-    @pl.when(swap_away)
+        pl.semaphore_signal(barrier, inc=1, device_id=cross_from, device_id_type=MESH)
+
+    @pl.when(swap_far)
     def _():
         pl.semaphore_signal(barrier, inc=1, device_id=swap_dev, device_id_type=MESH)
 
-    pl.semaphore_wait(barrier, CTX - 1 + 3 + cross_away.astype(jnp.int32) + swap_away.astype(jnp.int32))
+    pl.semaphore_wait(barrier, CTX - 1 + 3 + cross_group.astype(jnp.int32) + swap_far.astype(jnp.int32))
 
     def tok_gather(k):
         def rows(shard, half):
@@ -174,10 +178,10 @@
     t_g = [tok_gather(k) for k in range(2)]
     t_g[0].send("Bp", "Bm")
 
-    def w_slot(shard):
+    def w_slot(shard, turns=1):
         dz = {OWN_S: 0, PAIR_S: 0, LEFT: 3, RIGHT: 1, PLEFT: 3, PRIGHT: 1, FAR: 2, PFAR: 2}[shard]
         dy = 1 if shard in (PAIR_S, PLEFT, PRIGHT, PFAR) else 0
-        return rel_slot((z + dz + 4 - x) % 4, (y_lo + dy + y_hi) % 2)
+        return rel_slot((z + dz + 8 - turns * x) % 4, (y_lo + dy + y_hi) % 2)
 
     def w_lanes(shard, c):
         return pl.ds(pl.multiple_of(w_slot(shard) * ROWS + c * WROWS, WROWS), WROWS)
@@ -220,7 +224,7 @@
     w_sib(OWN_S)
 
     def ow_view(shard, half, c=core):
-        lanes = pl.ds(pl.multiple_of(w_slot(shard) * HALF, HALF), HALF)
+        lanes = pl.ds(pl.multiple_of(w_slot(shard, 2) * HALF, HALF), HALF)
         rows = pl.ds(pl.multiple_of(c * WROWS, WROWS), WROWS)
         if half is None:
             return ow_all.at[:, rows, lanes]
@@ -239,7 +243,7 @@
         device_id_type=MESH,
     )
 
-    swap_lanes = pl.ds(pl.multiple_of(rel_slot((x + 4 - z) % 4, (y_hi + y_lo) % 2) * HALF, HALF), HALF)
+    swap_lanes = pl.ds(pl.multiple_of(rel_slot((2 * x + 4 - z) % 4, (y_hi + y_lo) % 2) * HALF, HALF), HALF)
     swap_rows = pl.ds(pl.multiple_of(core * WROWS, WROWS), WROWS)
     swap = pltpu.make_async_remote_copy(
         src_ref=ow_held,
@@ -350,9 +354,9 @@
 
     early, late = 6 * ROWS, 2 * ROWS
 
-    @pl.loop(0, 12)
+    @pl.loop(0, 8)
     def _(i):
-        s, lanes = i // 4, pl.ds(pl.multiple_of((i % 4) * 256, 256), 256)
+        s, lanes = 1 + i // 4, pl.ds(pl.multiple_of((i % 4) * 256, 256), 256)
         acc[s, :, lanes] = dot(w_all[s, :, pl.ds(0, early)], tok_all[pl.ds(0, early), lanes])
 
     def forward(c):
@@ -365,16 +369,6 @@
             turned.append(jnp.concatenate([re * cos + im * sin, im * cos - re * sin], axis=1).astype(BF16))
         return dot(jnp.concatenate(turned, axis=0), f2[...])
 
-    @pl.loop(0, CTX)
-    def _(s):
-        ref = frecv.at[s]
-        pltpu.make_async_copy(ref, ref, f_rs.at[s]).wait()
-        xf[:, pl.ds(pl.multiple_of(s * 8, 8), 8), :] = frecv[s].astype(F32).reshape(OWN, 8, SIDE)
-
-    @pl.loop(0, OWN // 2, unroll=4)
-    def _(i):
-        spec[i] = forward(2 * i)
-
     for g in t_g:
         g.recv("Dp", "Dm", "Ep", "Em")
 
@@ -394,19 +388,22 @@
             w_all[s, :, pl.ds(early, late)], tok_all[pl.ds(early, late), lanes]
         )
 
-    @pl.loop(0, 3)
+    def halo_copy(first, count, i):
+        return pltpu.make_async_remote_copy(
+            src_ref=halo_send.at[pl.ds(first, count)],
+            dst_ref=halo_recv.at[pl.ds(first, count), pl.ds(SIDE - 8, 8)],
+            send_sem=halo_sem.at[2 * i],
+            recv_sem=halo_sem.at[2 * i + 1],
+            device_id=((ctx + 1) % CTX, tp),
+            device_id_type=MESH,
+        )
+
+    @pl.loop(1, 3)
     def _(s):
         finish_tile(s, 3)
         halo_send[s] = acc[s, :, pl.ds(SLAB - SIDE, SIDE)].T[SIDE - 8 :]
 
-    halo = pltpu.make_async_remote_copy(
-        src_ref=halo_send,
-        dst_ref=halo_recv.at[:, pl.ds(SIDE - 8, 8)],
-        send_sem=halo_sem.at[0],
-        recv_sem=halo_sem.at[1],
-        device_id=((ctx + 1) % CTX, tp),
-        device_id_type=MESH,
-    )
+    halo = halo_copy(1, 2, 0)
     halo.start()
 
     @pl.loop(0, 6)
@@ -414,7 +411,7 @@
         finish_tile(1 + i // 3, i % 3)
 
     halo.wait_recv()
-    for s in range(3):
+    for s in (1, 2):
         halo_t[s] = jnp.where(ctx > 0, halo_recv[s].T, 0.0)
 
     def short(s, r0):
@@ -454,14 +451,24 @@
         copy.start()
         sib_sent.append(copy)
 
-    @pl.loop(0, 3)
+    @pl.loop(0, 4)
     def _(n):
-        finish_tile(0, n)
-
-    @pl.loop(0, ROWS // SUB)
-    def _(b):
-        r0 = pl.multiple_of(b * SUB, SUB)
-        acc[0, pl.ds(r0, SUB), :] = short(0, r0)
+        lanes = pl.ds(pl.multiple_of((3 - n) * 256, 256), 256)
+        acc[0, :, lanes] = dot(w_all[0], tok_all[:, lanes])
+
+    halo_send[0] = acc[0, :, pl.ds(SLAB - SIDE, SIDE)].T[SIDE - 8 :]
+    halo_zero = halo_copy(0, 1, 1)
+    halo_zero.start()
+
+    @pl.loop(0, CTX)
+    def _(s):
+        ref = frecv.at[s]
+        pltpu.make_async_copy(ref, ref, f_rs.at[s]).wait()
+        xf[:, pl.ds(pl.multiple_of(s * 8, 8), 8), :] = frecv[s].astype(F32).reshape(OWN, 8, SIDE)
+
+    @pl.loop(0, OWN // 2, unroll=4)
+    def _(i):
+        spec[i] = forward(2 * i)
 
     def take(h):
         part = pl.ds(h * SUB, SUB)
@@ -518,6 +525,12 @@
 
     h_g = [hid_gather(i) for i in range(len(PIECES))]
 
+    def last_stream(h):
+        @pl.loop(0, CTX)
+        def _(d):
+            r0 = pl.multiple_of(d * OWN + h * SUB, SUB)
+            acc[0, pl.ds(r0, SUB), :] = short(0, r0)
+
     def hidden(h):
         @pl.loop(0, CTX)
         def _(d):
@@ -537,6 +550,9 @@
     ow_g.send("A", "Bp", "Bm")
     ow_sib(OWN_S)
     convolve(1)
+    halo_zero.wait_recv()
+    halo_t[0] = jnp.where(ctx > 0, halo_recv[0].T, 0.0)
+    last_stream(0)
     hidden(0)
     h_g[0].send("A", "Bp", "Bm")
     ow_g.recv("Bp", "Bm")
@@ -546,6 +562,7 @@
     ow_g.recv("A")
     ow_g.send("Cp", "Cm")
     ow_sib(PAIR_S)
+    last_stream(1)
     hidden(1)
     h_g[2].send("Bp", "Bm", "A")
     h_g[1].send("A", "Bp", "Bm")
@@ -616,6 +633,7 @@
         swap.wait_send()
 
     halo.wait_send()
+    halo_zero.wait_send()
 
     @pl.loop(0, CTX)
     def _(d):
@@ -668,7 +686,7 @@
             dma((8,)), dma((8,)),
             dma((8,)), dma((8,)),
             dma((4,)),
-            dma((2,)),
+            dma((4,)),
             dma((CTX,)), dma((CTX,)),
             dma((PART, CTX)), dma((PART, CTX)),
             dma((PART, CTX)), dma((PART, CTX)),

time: 189 us -> 185 us (0.979)
  the two profiles are of different devices: /device:TPU:106 before, /device:TPU:1 now
where the time goes in v3:
time: 185 us
  Pallas kernels  183 us (99%)
  local copies, waits for them, and re-layouts  2.26 us (1%)
    pallas_call x1, Pallas kernels, per_device(): pl.pallas_call(kernel, out_shape=jax.ShapeDtypeStruct((ROWS, SLAB), BF16)...  183 us

profile of v3, /device:TPU:1, one launch (start us, length us, event | category | flops | bytes accessed | tf_op | source)
XLA Modules:
  0.0 184.9 jit_solution(12249580659949200453)
XLA Ops:
  0.0 182.6 %hyena.1 = bf16[512,1024]{1,0:T(8,128)(2,1)} custom-call(bf16[512,1024]{1,0:T(8,128)(2,1)} %tok.1, bf16[3,256,512]{2,1,0:T(8,128)(2,1)} %w.1, f32[3,3,512]{2,1,0:T(4,128)} %bitcast.2, f32[512,1024]{1,0:T(8,128)} %filt.1, f32[1,512]{1,0:T(1,128)} %bitcast.3, bf16[512,256]{1,0:T(8,128)(2,1)} %ow.1, bf16[256,128]{1,0:T(8,128)(2,1)} %constant.10.clone.f1, ...), custom_call_target="tpu_custom_call" | custom-call | flops 19579869184 | bytes 8388608 | tf_op jit(solution)/shard_map/hyena/pallas_call | solution.py:652
  182.6 2.3 %copy.13 = bf16[512,1024]{1,0:T(8,128)(2,1)} copy(bf16[512,1024]{1,0:T(8,128)(2,1)} %hyena.1) | data formatting | bytes 2097152

commit v4 on v3

--- a/solution.py
+++ b/solution.py
@@ -372,16 +372,6 @@
     for g in t_g:
         g.recv("Dp", "Dm", "Ep", "Em")
 
-    pltpu.make_async_copy(ow_held, ow_held, swap_sem.at[1]).wait()
-
-    @pl.when(swap_away)
-    def _():
-        swap.start()
-
-    @pl.when(jnp.logical_not(swap_away))
-    def _():
-        pltpu.make_async_copy(ow_held, ow_view(OWN_S, None), swap_sem.at[3]).start()
-
     def finish_tile(s, n):
         lanes = pl.ds(pl.multiple_of(n * 256, 256), 256)
         acc[s, :, lanes] = acc[s, :, lanes] + dot(
@@ -429,7 +419,7 @@
 
     for h in range(PART):
 
-        @pl.loop(0, CTX)
+        @pl.loop(0, CTX, unroll=2)
         def _(d):
             r0 = pl.multiple_of(d * OWN + h * SUB, SUB)
             g = (short(1, r0) * short(2, r0)).astype(BF16)
@@ -451,6 +441,16 @@
         copy.start()
         sib_sent.append(copy)
 
+    pltpu.make_async_copy(ow_held, ow_held, swap_sem.at[1]).wait()
+
+    @pl.when(swap_away)
+    def _():
+        swap.start()
+
+    @pl.when(jnp.logical_not(swap_away))
+    def _():
+        pltpu.make_async_copy(ow_held, ow_view(OWN_S, None), swap_sem.at[3]).start()
+
     @pl.loop(0, 4)
     def _(n):
         lanes = pl.ds(pl.multiple_of((3 - n) * 256, 256), 256)
@@ -482,7 +482,7 @@
     def convolve(h):
         part = pl.ds(h * SUB, SUB)
 
-        @pl.loop(0, SUB // 2, unroll=4)
+        @pl.loop(0, SUB // 2, unroll=8)
         def _(i):
             c = h * SUB + 2 * i
             x_f, h_f = forward(c), spec[h * (SUB // 2) + i]
@@ -526,7 +526,7 @@
     h_g = [hid_gather(i) for i in range(len(PIECES))]
 
     def last_stream(h):
-        @pl.loop(0, CTX)
+        @pl.loop(0, CTX, unroll=2)
         def _(d):
             r0 = pl.multiple_of(d * OWN + h * SUB, SUB)
             acc[0, pl.ds(r0, SUB), :] = short(0, r0)

time: 185 us -> 185 us (level)
  no operation moved by 1% of the time
where the time goes in v4:
time: 185 us
  Pallas kernels  182 us (98%)
  local copies, waits for them, and re-layouts  2.26 us (1%)
    pallas_call x1, Pallas kernels, per_device(): pl.pallas_call(kernel, out_shape=jax.ShapeDtypeStruct((ROWS, SLAB), BF16)...  182 us

profile of v4, /device:TPU:1, one launch (start us, length us, event | category | flops | bytes accessed | tf_op | source)
XLA Modules:
  0.0 184.6 jit_solution(14393462799334673830)
XLA Ops:
  0.0 182.4 %hyena.1 = bf16[512,1024]{1,0:T(8,128)(2,1)} custom-call(bf16[512,1024]{1,0:T(8,128)(2,1)} %tok.1, bf16[3,256,512]{2,1,0:T(8,128)(2,1)} %w.1, f32[3,3,512]{2,1,0:T(4,128)} %bitcast.2, f32[512,1024]{1,0:T(8,128)} %filt.1, f32[1,512]{1,0:T(1,128)} %bitcast.3, bf16[512,256]{1,0:T(8,128)(2,1)} %ow.1, bf16[256,128]{1,0:T(8,128)(2,1)} %constant.10.clone.f1, ...), custom_call_target="tpu_custom_call" | custom-call | flops 19579869184 | bytes 8388608 | tf_op jit(solution)/shard_map/hyena/pallas_call | solution.py:652
  182.4 2.3 %copy.13 = bf16[512,1024]{1,0:T(8,128)(2,1)} copy(bf16[512,1024]{1,0:T(8,128)(2,1)} %hyena.1) | data formatting | bytes 2097152
